TPU v7x, 32 devices: a whole 2x2x4 slice. The times are simulated.
32 devices in a mesh: val: 4 (over y, x), col: 8 (over z, core).
Axes of the slice: x: 2, y: 2, z: 4, core: 2. Of those that a mesh axis runs over, the one named last changes fastest.
Arguments:
- valence_store: float32 [4, 8, 2, 48, 2304], P('val', 'col'), may hold values from -6 to 6
- band_owner: int32 [4], replicated, may hold values from 0 to 7
- valence_energy: float32 [4], P('val'), may hold values from -8 to -1
- cond_bands: float32 [32, 2, 48, 2304], P('col'), may hold values from -6 to 6
- cond_energy: float32 [32], P('col'), may hold values from 0.5 to 10
- gvec_index: int32 [4096], replicated, may hold values from 0 to 110591, as said below
Outputs:
- chi_zero: float32 [2, 256, 4096], P(None, 'val', 'col')
Inputs may be any that keep to these rules, and one draw needn't show every extreme that they name: `gvec_index`: distinct grid indices; entry 0 is 0 (the zero vector) and entry 1 is 110591.
All inputs are finite; a program needn't handle non-finite values.
Results may differ from a plain program's by a relative error of at most 0.0038.
Values may be sent and summed in bfloat16 or wider, within the bound.
A program may use at most 256 MiB of HBM per device.

v0:
```python
import functools
import math

import jax
import jax.numpy as jnp
import ml_dtypes
import numpy as np
from jax import lax
from jax.experimental import pallas as pl
from jax.experimental.pallas import tpu as pltpu
from jax.sharding import PartitionSpec as P

ROW_DEV = 64
LANES = 128
BF16 = jnp.bfloat16
F32 = jnp.float32


def split_table(table):
    high = table.astype(ml_dtypes.bfloat16)
    low = (table - high.astype(np.float64)).astype(ml_dtypes.bfloat16)
    return high, low


def tables(side):
    counter = np.arange(side)
    angles = 2.0 * math.pi * ((counter[:, None] * counter[None, :]) % side) / side
    cosine, sine = np.cos(angles), np.sin(angles)
    first = np.zeros((2, 2, side, 2, LANES))
    for band in range(2):
        span = slice(band * side, (band + 1) * side)
        first[band, 0, :, 0, span] = cosine
        first[band, 1, :, 0, span] = sine
        first[band, 1, :, 1, span] = cosine
        first[band, 0, :, 1, span] = -sine
    first_high, first_low = split_table(first.reshape(4 * side, 2 * LANES))
    both_high, both_low = split_table(np.concatenate([cosine, sine], 0))
    left = np.concatenate([both_high, both_high, both_low], 1)
    return first_high, first_low, left


def picker(side, pairs):
    table = np.zeros((2, pairs, LANES, LANES))
    for part in range(2):
        for pair in range(pairs):
            for band in range(2):
                table[part, pair, band * side : (band + 1) * side, (part * pairs + pair) * 2 + band] = 1.0
    return table.reshape(2 * pairs * LANES, LANES).astype(ml_dtypes.bfloat16)


def split(value):
    high = value.astype(BF16)
    return high, (value - high.astype(F32)).astype(BF16)


def dot(left, right, dims=((1,), (0,))):
    return lax.dot_general(left, right, (dims, ((), ())), preferred_element_type=F32)


def spectrum_kernel(
    side, rows_ref, valence_ref, cond_ref, first_high_ref, first_low_ref, left_ref,
    picker_ref, kx_ref, scale_ref, out_ref, grid_a, grid_b, spots, chosen,
):
    bands = cond_ref.shape[0]
    pairs = bands // 2
    plane = side * side
    half = pairs * LANES
    width = 256

    for pair in range(pairs):
        @pl.loop(0, plane // width)
        def _(step, pair=pair):
            lanes = pl.ds(pl.multiple_of(step * width, width), width)
            v_re, v_im = valence_ref[0, :, lanes], valence_ref[1, :, lanes]
            parts = []
            for band in (2 * pair, 2 * pair + 1):
                c_re, c_im = cond_ref[band, 0, :, lanes], cond_ref[band, 1, :, lanes]
                parts += [v_re * c_re + v_im * c_im, v_re * c_im - v_im * c_re]
            high, low = split(jnp.concatenate(parts, 0).T)
            result = (
                dot(high, first_high_ref[...])
                + dot(low, first_high_ref[...])
                + dot(high, first_low_ref[...])
            )
            rows = pl.ds(pl.multiple_of(step * width, width), width)
            grid_a[rows, pair * LANES : (pair + 1) * LANES] = result[:, :LANES]
            grid_a[rows, half + pair * LANES : half + (pair + 1) * LANES] = result[:, LANES:]

    def turn(block):
        high, low = split(block)
        both = dot(left_ref[...], jnp.concatenate([high, low, high], 0))
        real = both[:side, :half] + both[side:, half:]
        imag = both[:side, half:] - both[side:, :half]
        return real, imag

    @pl.loop(0, side)
    def _(y):
        rows = pl.ds(pl.multiple_of(y * side, side), side)
        real, imag = turn(grid_a[rows, :])
        for pair in range(pairs):
            span = slice(pair * LANES, (pair + 1) * LANES)
            grid_b[pair, rows, :] = real[:, span]
            grid_b[pairs + pair, rows, :] = imag[:, span]

    @pl.loop(0, side)
    def _(kz):
        block = jnp.concatenate(
            [grid_b[part, pl.ds(kz, side, stride=side), :] for part in range(2 * pairs)], 1
        )
        real, imag = turn(block)
        for pair in range(pairs):
            span = slice(pair * LANES, (pair + 1) * LANES)
            base = kz * side * 8
            spots[pl.ds(base + pair, side, stride=8), :] = real[:, span]
            spots[pl.ds(base + pairs + pair, side, stride=8), :] = imag[:, span]

    count = out_ref.shape[1]
    chunk = 512
    lane = lax.broadcasted_iota(jnp.int32, (1, LANES), 1)
    lane = jnp.where(lane < side, lane, jnp.where(lane < 2 * side, lane - side, -1)).astype(F32)

    @pl.loop(0, count // chunk)
    def _(step):
        base = step * chunk

        @pl.loop(0, chunk // 32)
        def _(inner):
            for item in range(32):
                spot = pl.multiple_of(rows_ref[base + inner * 32 + item] * 8, 8)
                to = pl.multiple_of((inner * 32 + item) * 8, 8)
                chosen[pl.ds(to, 8), :] = spots[pl.ds(spot, 8), :]

        where = pl.ds(pl.multiple_of(base, chunk), chunk)
        wanted = jnp.broadcast_to(kx_ref[:, where], (LANES, chunk)).T
        mask = wanted == lane
        total = jnp.zeros((chunk, LANES), F32)
        for part in range(2 * pairs):
            value = jnp.where(mask, chosen[pl.ds(part, chunk, stride=8), :], 0.0)
            high, low = split(value)
            table = picker_ref[part * LANES : (part + 1) * LANES, :]
            total += dot(high, table) + dot(low, table)
        values = total.T[: out_ref.shape[0], :]
        out_ref[:, where] = (values * scale_ref[:, :1]).astype(BF16)


def pair_elements(valence, cond_bands, scaling, gvec_index):
    bands, _, side, plane = cond_bands.shape
    count = gvec_index.shape[0]
    pairs = bands // 2
    first_high, first_low, left = tables(side)
    spot = gvec_index % side * side + gvec_index // side % side
    kx = (gvec_index // plane).astype(F32)[None, :]
    scale = jnp.broadcast_to(jnp.tile(scaling, 2)[:, None], (2 * bands, LANES))
    vmem = pl.BlockSpec(memory_space=pltpu.VMEM)
    return pl.pallas_call(
        functools.partial(spectrum_kernel, side),
        out_shape=jax.ShapeDtypeStruct((2 * bands, count), BF16),
        in_specs=[pl.BlockSpec(memory_space=pltpu.SMEM)] + [vmem] * 8,
        out_specs=vmem,
        scratch_shapes=[
            pltpu.VMEM((plane, 2 * pairs * LANES), F32),
            pltpu.VMEM((2 * pairs, plane, LANES), F32),
            pltpu.VMEM((plane * 8, LANES), F32),
            pltpu.VMEM((512 * 8, LANES), F32),
        ],
        compiler_params=pltpu.CompilerParams(vmem_limit_bytes=48 * 1024 * 1024),
    )(spot, valence, cond_bands, first_high, first_low, left, picker(side, pairs), kx, scale)


def from_root(block, axis, source):
    block = jnp.where(lax.axis_index(axis) == source, block, jnp.zeros_like(block))
    return lax.psum(block, axis)


def local(valence_store, band_owner, valence_energy, cond_bands, cond_energy, gvec_index):
    bands, _, side, plane = cond_bands.shape
    n_val, n_col = lax.axis_size("val"), lax.axis_size("col")
    owner_index = band_owner[lax.axis_index("val")]
    valence = from_root(valence_store[0, 0], "col", owner_index)
    constant = (bands * n_col * n_val) ** (-0.25) * side ** (-1.5)
    scaling = jnp.sqrt(2.0 / (cond_energy - valence_energy[0])) * constant
    picked = pair_elements(valence, cond_bands, scaling, gvec_index)
    count = picked.shape[1]
    cols = count // n_col
    columns = picked.reshape(2 * bands, n_col, cols).transpose(1, 0, 2)
    columns = jnp.broadcast_to(columns[None], (n_val, n_col, 2 * bands, cols))
    rows = picked[:, : ROW_DEV * n_val].reshape(2 * bands, n_val, ROW_DEV).transpose(1, 0, 2)
    rows = jnp.broadcast_to(rows[:, None], (n_val, n_col, 2 * bands, ROW_DEV))
    message = jnp.concatenate([columns, rows], 3).reshape(n_val * n_col, 2 * bands, cols + ROW_DEV)
    message = lax.all_to_all(message, ("val", "col"), split_axis=0, concat_axis=0, tiled=True)
    message = message.reshape(n_val * n_col, 2, bands, cols + ROW_DEV).transpose(1, 0, 2, 3)
    message = message.reshape(2, n_val * n_col * bands, cols + ROW_DEV)
    columns, rows = message[:, :, :cols], message[:, :, cols:]
    row_re, row_im = rows[0], rows[1]
    both = jnp.concatenate([rows[0], rows[1]], 0)
    turned = jnp.concatenate([rows[1], -rows[0]], 0)
    flat = columns.reshape(-1, cols)
    return -jnp.stack([dot(both, flat, ((0,), (0,))), dot(turned, flat, ((0,), (0,)))])


def solution(mesh):
    return jax.shard_map(
        local,
        mesh=mesh,
        in_specs=(
            P("val", "col", None, None, None),
            P(),
            P("val"),
            P("col", None, None, None),
            P("col"),
            P(),
        ),
        out_specs=P(None, "val", "col"),
        check_vma=False,
    )
```

profile of v0, /device:TPU:0, one launch (start us, length us, event | category | flops | bytes accessed | tf_op | source)
XLA Modules:
  0.0 136.8 jit_solution(1109635814636639622)
XLA Ops:
  6.5 0.0 all-reduce.2.cloned.1.call-start
  6.5 1.2 dynamic_slice.3
  8.4 1.0 select_bitcast_fusion
  9.4 0.0 all-reduce.2.cloned.1.call-update
  10.1 0.7 sqrt_multiply_fusion
  10.8 0.1 broadcast_in_dim.27
  10.9 0.8 fusion.9
  11.6 58.1 %all-reduce.2.cloned.1.call-done.valence_ref = f32[2,48,2304]{2,1,0:T(8,128)} async-done(((f32[2,48,2304]{2,1,0:T(8,128)}), f32[2,48,2304]{2,1,0:T(8,128)}) %all-reduce.2.cloned.1.call-update) | async-done | bytes 884752 | tf_op jit(solution)/shard_map/psum | solution.py:172
  69.8 0.1 broadcast_in_dim.28.scale_ref
  69.8 0.0 copy-start
  69.8 2.0 %copy-done = f32[4,2,48,2304]{3,2,1,0:T(8,128)S(1)} copy-done((f32[4,2,48,2304]{3,2,1,0:T(8,128)S(1)}, f32[4,2,48,2304]{3,2,1,0:T(8,128)}, u32[]{:S(2)}) %copy-start) | copy-done | bytes 3538968
  71.8 0.0 copy-start.1
  71.8 1.2 copy-done.1
  73.0 0.0 copy-start.2
  73.0 0.9 copy-done.2
  73.9 0.0 copy-start.3
  73.9 0.9 copy-done.3
  74.8 0.0 copy-start.4
  74.8 0.9 copy-done.4
  75.7 0.0 copy-start.5
  75.7 0.8 copy-done.5
  76.5 35.0 %shard_map.100 = bf16[8,4096]{1,0:T(8,128)(2,1)S(1)} custom-call(s32[4096]{0:T(1024)S(1)} %get-tuple-element.8.rows_ref, f32[2,48,2304]{2,1,0:T(8,128)S(1)} %copy-done.1, f32[4,2,48,2304]{3,2,1,0:T(8,128)S(1)} %copy-done, bf16[192,256]{1,0:T(8,128)(2,1)S(1)} %copy-done.3, bf16[192,256]{1,0:T(8,128)(2,1)S(1)} %copy-done.4, bf16[96,144]{1,0:T(8,128)(2,1)S(1)} %copy-done.5, ...), custom_call_target="tpu_custom_call" | custom-call | tf_op jit(solution)/shard_map/pallas_call | solution.py:155
  111.5 0.1 reshape.26
  111.7 16.3 %all_to_all.5 = bf16[32,8,576]{2,1,0:T(8,128)(2,1)S(1)} all-to-all(bf16[32,8,576]{2,1,0:T(8,128)(2,1)S(1)} %bitcast.31), channel_id=1, replica_groups=mesh['val'=4,'col'=8] {'val','col'}, dimensions={0} | all-to-all | bytes 589824 | tf_op jit(solution)/shard_map/all_to_all | solution.py:190
  128.0 0.3 copy.27
  128.4 0.1 fusion.13
  128.5 0.2 slice.24
  128.7 0.1 copy.28
  128.8 0.1 copy.29
  128.9 0.2 convolution_bitcast_fusion.1
  129.1 0.2 convolution_bitcast_fusion
  129.3 0.7 maximum_negate_fusion
  (9 shorter events, 0.2 us)
Async XLA Ops:
  6.5 63.2 %all-reduce.2.cloned.1.call-start = ((), (), s32[]{:S(2)}) async-start(), calls=%async_computation.1 | async-start | bytes 1769472 | tf_op jit(solution)/shard_map/psum | solution.py:172
  69.8 2.0 %copy-start = (f32[4,2,48,2304]{3,2,1,0:T(8,128)S(1)}, f32[4,2,48,2304]{3,2,1,0:T(8,128)}, u32[]{:S(2)}) copy-start(f32[4,2,48,2304]{3,2,1,0:T(8,128)} %cond_ref.1) | copy-start | bytes 10616836
  71.8 1.2 copy-start.1
  73.0 0.9 copy-start.2
  73.9 0.9 copy-start.3
  74.8 0.9 copy-start.4
  75.7 0.8 copy-start.5
Sparse Core Ops, SparseCore 0:
  9.7 59.9 all-reduce.1
where the time goes:
time: 137 us
  waiting for transfers between devices  58.1 us (42%)
  Pallas kernels  35 us (26%)
  blocking collectives  16.3 us (12%)
  between operations  14.8 us (11%)
  local copies, waits for them, and re-layouts  9.06 us (7%)
  other arithmetic  3.22 us (2%)
    psum x1, waiting for transfers between devices, from_root(): return lax.psum(block, axis)  58.1 us
    pallas_call x1, Pallas kernels, pair_elements(): pl.pallas_call(functools.partial(spectrum_kernel, side), out_shape=jax.Sh...  35 us
    all_to_all x1, blocking collectives, local(): lax.all_to_all(message, ('val', 'col'), split_axis=0, concat_axis=0, tile...  16.3 us
    unnamed x12, local copies, waits for them, and re-layouts  6.65 us
  transfers between devices with their start and end apart: 1, of which 1 were waited for; matrix products, arithmetic and copies ran while one was open for 1% of the time, Pallas kernels for 0%

commit v1 on v0

--- a/solution.py
+++ b/solution.py
@@ -12,6 +12,8 @@
 
 ROW_DEV = 64
 LANES = 128
+WIDTH = 256
+MESH = pl.DeviceIdType.MESH
 BF16 = jnp.bfloat16
 F32 = jnp.float32
 
@@ -58,20 +60,96 @@
 
 
 def spectrum_kernel(
-    side, rows_ref, valence_ref, cond_ref, first_high_ref, first_low_ref, left_ref,
-    picker_ref, kx_ref, scale_ref, out_ref, grid_a, grid_b, spots, chosen,
+    side, scale_constant, rows_ref, owner_ref, val_energy_ref, energy_ref, store_ref, cond_hbm,
+    first_high_ref, first_low_ref, left_ref, picker_ref, kx_ref, out_ref,
+    grid_a, grid_b, spots, chosen, cond_ref, streams, mine, valence_ref,
+    send_sems, recv_sems, cond_sem,
 ):
     bands = cond_ref.shape[0]
     pairs = bands // 2
     plane = side * side
     half = pairs * LANES
-    width = 256
-
-    for pair in range(pairs):
-        @pl.loop(0, plane // width)
-        def _(step, pair=pair):
-            lanes = pl.ds(pl.multiple_of(step * width, width), width)
-            v_re, v_im = valence_ref[0, :, lanes], valence_ref[1, :, lanes]
+    chunks = plane // WIDTH
+
+    cond_copy = pltpu.make_async_copy(cond_hbm, cond_ref, cond_sem)
+    cond_copy.start()
+
+    n_col = lax.axis_size("col")
+    me = lax.axis_index("col")
+    chips = n_col // 2
+    chip, core = me // 2, me % 2
+    sibling = me + 1 - 2 * core
+    right = jnp.minimum(me + 2, n_col - 2 + core)
+    left = jnp.maximum(me - 2, core)
+    has_left, has_right = chip > 0, chip < chips - 1
+
+    barrier = pltpu.get_barrier_semaphore()
+    pl.semaphore_signal(barrier, inc=1, device_id={"col": sibling}, device_id_type=MESH)
+
+    @pl.when(has_left)
+    def _():
+        pl.semaphore_signal(barrier, inc=1, device_id={"col": left}, device_id_type=MESH)
+
+    @pl.when(has_right)
+    def _():
+        pl.semaphore_signal(barrier, inc=1, device_id={"col": right}, device_id_type=MESH)
+
+    pl.semaphore_wait(barrier, 3 - (chip == 0).astype(jnp.int32) - (chip == chips - 1).astype(jnp.int32))
+
+    def copy(kind, k):
+        peer = (sibling, right, left)[kind]
+        return pltpu.make_async_remote_copy(
+            src_ref=streams.at[kind, 0, k],
+            dst_ref=streams.at[kind, 1, k],
+            send_sem=send_sems.at[kind, k],
+            recv_sem=recv_sems.at[kind, k],
+            device_id={"col": peer},
+            device_id_type=MESH,
+        )
+
+    def final_copy(part, k):
+        return pltpu.make_async_remote_copy(
+            src_ref=valence_ref.at[part, k],
+            dst_ref=valence_ref.at[part, k],
+            send_sem=send_sems.at[3, k],
+            recv_sem=recv_sems.at[3, k],
+            device_id={"col": sibling},
+            device_id_type=MESH,
+        )
+
+    def lanes_of(k):
+        return pl.ds(pl.multiple_of(k * WIDTH, WIDTH), WIDTH)
+
+    gap = jnp.full((1, WIDTH), owner_ref[lax.axis_index("val")] - me).astype(F32)
+    owned = jnp.maximum(1.0 - gap * gap, 0.0)
+
+    @pl.loop(0, chunks)
+    def _(k):
+        streams[0, 0, k] = store_ref[1 - core, :, lanes_of(k)] * owned
+        copy(0, k).start()
+
+    @pl.when(jnp.logical_not(has_left))
+    def _():
+        streams[1, 1] = jnp.zeros((chunks, side, WIDTH), F32)
+
+    @pl.when(jnp.logical_not(has_right))
+    def _():
+        streams[2, 1] = jnp.zeros((chunks, side, WIDTH), F32)
+
+    def pass_on(kind, k, has_source, has_target):
+        @pl.when(has_source)
+        def _():
+            copy(kind, k).wait_recv()
+
+        @pl.when(has_target)
+        def _():
+            streams[kind, 0, k] = mine[k] + streams[kind, 1, k]
+            copy(kind, k).start()
+
+    def first_axis(k):
+        v_re, v_im = valence_ref[0, k], valence_ref[1, k]
+        lanes = lanes_of(k)
+        for pair in range(pairs):
             parts = []
             for band in (2 * pair, 2 * pair + 1):
                 c_re, c_im = cond_ref[band, 0, :, lanes], cond_ref[band, 1, :, lanes]
@@ -82,9 +160,8 @@
                 + dot(low, first_high_ref[...])
                 + dot(high, first_low_ref[...])
             )
-            rows = pl.ds(pl.multiple_of(step * width, width), width)
-            grid_a[rows, pair * LANES : (pair + 1) * LANES] = result[:, :LANES]
-            grid_a[rows, half + pair * LANES : half + (pair + 1) * LANES] = result[:, LANES:]
+            grid_a[lanes, pair * LANES : (pair + 1) * LANES] = result[:, :LANES]
+            grid_a[lanes, half + pair * LANES : half + (pair + 1) * LANES] = result[:, LANES:]
 
     def turn(block):
         high, low = split(block)
@@ -93,14 +170,50 @@
         imag = both[:side, half:] - both[side:, :half]
         return real, imag
 
-    @pl.loop(0, side)
-    def _(y):
-        rows = pl.ds(pl.multiple_of(y * side, side), side)
+    def last_axis(y):
+        rows = pl.ds(pl.multiple_of(y * side, 8), side)
         real, imag = turn(grid_a[rows, :])
         for pair in range(pairs):
             span = slice(pair * LANES, (pair + 1) * LANES)
             grid_b[pair, rows, :] = real[:, span]
             grid_b[pairs + pair, rows, :] = imag[:, span]
+
+    lag = max(1, chips // 2)
+    near_left = chip < chips // 2
+    right_lag = jnp.where(near_left, 0, lag)
+    left_lag = lag - right_lag
+    cond_copy.wait()
+
+    @pl.loop(0, chunks + lag + 1)
+    def _(step):
+        @pl.when(step < chunks)
+        def _():
+            copy(0, step).wait_recv()
+            mine[step] = streams[0, 1, step] + store_ref[core, :, lanes_of(step)] * owned
+
+        @pl.when((step >= right_lag) & (step - right_lag < chunks))
+        def _():
+            pass_on(1, step - right_lag, has_left, has_right)
+
+        @pl.when((step >= left_lag) & (step - left_lag < chunks))
+        def _():
+            pass_on(2, step - left_lag, has_right, has_left)
+
+        @pl.when((step >= lag) & (step - lag < chunks))
+        def _():
+            k = step - lag
+            valence_ref[core, k] = mine[k] + streams[1, 1, k] + streams[2, 1, k]
+            final_copy(core, k).start()
+
+        @pl.when(step > lag)
+        def _():
+            k = step - lag - 1
+            final_copy(1 - core, k).wait_recv()
+            first_axis(k)
+
+            @pl.loop(k * WIDTH // side, (k + 1) * WIDTH // side)
+            def _(y):
+                last_axis(y)
 
     @pl.loop(0, side)
     def _(kz):
@@ -110,12 +223,17 @@
         real, imag = turn(block)
         for pair in range(pairs):
             span = slice(pair * LANES, (pair + 1) * LANES)
-            base = kz * side * 8
-            spots[pl.ds(base + pair, side, stride=8), :] = real[:, span]
-            spots[pl.ds(base + pairs + pair, side, stride=8), :] = imag[:, span]
+            base = kz * side
+            spots[pl.ds(base, side), pair, :] = real[:, span]
+            spots[pl.ds(base, side), pairs + pair, :] = imag[:, span]
 
     count = out_ref.shape[1]
     chunk = 512
+    row = lax.broadcasted_iota(jnp.int32, (2 * bands, LANES), 0) % bands
+    energy = jnp.zeros((2 * bands, LANES), F32)
+    for band in range(bands):
+        energy = jnp.where(row == band, energy_ref[band], energy)
+    scale = jnp.sqrt(2.0 / (energy - val_energy_ref[0])) * scale_constant
     lane = lax.broadcasted_iota(jnp.int32, (1, LANES), 1)
     lane = jnp.where(lane < side, lane, jnp.where(lane < 2 * side, lane - side, -1)).astype(F32)
 
@@ -126,60 +244,79 @@
         @pl.loop(0, chunk // 32)
         def _(inner):
             for item in range(32):
-                spot = pl.multiple_of(rows_ref[base + inner * 32 + item] * 8, 8)
-                to = pl.multiple_of((inner * 32 + item) * 8, 8)
-                chosen[pl.ds(to, 8), :] = spots[pl.ds(spot, 8), :]
+                chosen[inner * 32 + item] = spots[rows_ref[base + inner * 32 + item]]
 
         where = pl.ds(pl.multiple_of(base, chunk), chunk)
         wanted = jnp.broadcast_to(kx_ref[:, where], (LANES, chunk)).T
         mask = wanted == lane
         total = jnp.zeros((chunk, LANES), F32)
         for part in range(2 * pairs):
-            value = jnp.where(mask, chosen[pl.ds(part, chunk, stride=8), :], 0.0)
+            value = jnp.where(mask, chosen[:, part, :], 0.0)
             high, low = split(value)
             table = picker_ref[part * LANES : (part + 1) * LANES, :]
             total += dot(high, table) + dot(low, table)
         values = total.T[: out_ref.shape[0], :]
-        out_ref[:, where] = (values * scale_ref[:, :1]).astype(BF16)
-
-
-def pair_elements(valence, cond_bands, scaling, gvec_index):
+        out_ref[:, where] = (values * scale[:, :1]).astype(BF16)
+
+    @pl.loop(0, chunks)
+    def _(k):
+        copy(0, k).wait_send()
+        final_copy(core, k).wait_send()
+
+        @pl.when(has_right)
+        def _():
+            copy(1, k).wait_send()
+
+        @pl.when(has_left)
+        def _():
+            copy(2, k).wait_send()
+
+
+def pair_elements(store, owner, val_energy, cond_bands, cond_energy, gvec_index):
     bands, _, side, plane = cond_bands.shape
     count = gvec_index.shape[0]
     pairs = bands // 2
+    chunks = plane // WIDTH
     first_high, first_low, left = tables(side)
     spot = gvec_index % side * side + gvec_index // side % side
     kx = (gvec_index // plane).astype(F32)[None, :]
-    scale = jnp.broadcast_to(jnp.tile(scaling, 2)[:, None], (2 * bands, LANES))
+    total_bands = bands * lax.axis_size("col") * lax.axis_size("val")
+    constant = total_bands ** (-0.25) * side ** (-1.5)
     vmem = pl.BlockSpec(memory_space=pltpu.VMEM)
+    smem = pl.BlockSpec(memory_space=pltpu.SMEM)
     return pl.pallas_call(
-        functools.partial(spectrum_kernel, side),
+        functools.partial(spectrum_kernel, side, constant),
         out_shape=jax.ShapeDtypeStruct((2 * bands, count), BF16),
-        in_specs=[pl.BlockSpec(memory_space=pltpu.SMEM)] + [vmem] * 8,
+        in_specs=[smem] * 4 + [vmem, pl.BlockSpec(memory_space=pl.ANY)] + [vmem] * 5,
         out_specs=vmem,
         scratch_shapes=[
             pltpu.VMEM((plane, 2 * pairs * LANES), F32),
             pltpu.VMEM((2 * pairs, plane, LANES), F32),
-            pltpu.VMEM((plane * 8, LANES), F32),
-            pltpu.VMEM((512 * 8, LANES), F32),
+            pltpu.VMEM((plane, 2 * pairs, LANES), F32),
+            pltpu.VMEM((512, 2 * pairs, LANES), F32),
+            pltpu.VMEM(cond_bands.shape, F32),
+            pltpu.VMEM((3, 2, chunks, side, WIDTH), F32),
+            pltpu.VMEM((chunks, side, WIDTH), F32),
+            pltpu.VMEM((2, chunks, side, WIDTH), F32),
+            pltpu.SemaphoreType.DMA((4, chunks)),
+            pltpu.SemaphoreType.DMA((4, chunks)),
+            pltpu.SemaphoreType.DMA,
         ],
-        compiler_params=pltpu.CompilerParams(vmem_limit_bytes=48 * 1024 * 1024),
-    )(spot, valence, cond_bands, first_high, first_low, left, picker(side, pairs), kx, scale)
-
-
-def from_root(block, axis, source):
-    block = jnp.where(lax.axis_index(axis) == source, block, jnp.zeros_like(block))
-    return lax.psum(block, axis)
+        compiler_params=pltpu.CompilerParams(
+            vmem_limit_bytes=60 * 1024 * 1024, collective_id=0, has_side_effects=True
+        ),
+    )(
+        spot, owner, val_energy, cond_energy, store, cond_bands,
+        first_high, first_low, left, picker(side, pairs), kx,
+    )
 
 
 def local(valence_store, band_owner, valence_energy, cond_bands, cond_energy, gvec_index):
     bands, _, side, plane = cond_bands.shape
     n_val, n_col = lax.axis_size("val"), lax.axis_size("col")
-    owner_index = band_owner[lax.axis_index("val")]
-    valence = from_root(valence_store[0, 0], "col", owner_index)
-    constant = (bands * n_col * n_val) ** (-0.25) * side ** (-1.5)
-    scaling = jnp.sqrt(2.0 / (cond_energy - valence_energy[0])) * constant
-    picked = pair_elements(valence, cond_bands, scaling, gvec_index)
+    picked = pair_elements(
+        valence_store[0, 0], band_owner, valence_energy, cond_bands, cond_energy, gvec_index
+    )
     count = picked.shape[1]
     cols = count // n_col
     columns = picked.reshape(2 * bands, n_col, cols).transpose(1, 0, 2)

time: 137 us -> 121 us (0.88)
  Pallas kernels: 35 us -> 99 us
  waiting for transfers between devices: 58.1 us -> 0 us
  between operations: 14.8 us -> 0.76 us
  local copies, waits for them, and re-layouts: 9.06 us -> 2.51 us
    pallas_call x1, Pallas kernels: 35 us -> 99 us  [pair_elements(): pl.pallas_call(functools.partial(spectrum_kernel, side, constant), out_sh...]
    psum x1 -> x0, waiting for transfers between devices: 58.1 us -> none  [from_root(): return lax.psum(block, axis)]
    unnamed x12 -> x0, local copies, waits for them, and re-layouts: 6.65 us -> none
  transfers between devices with their start and end apart: 1 -> 0, of which waited for: 1 -> 0; matrix products, arithmetic and copies ran while one was open for 1% -> 0% of each run, Pallas kernels for 0% -> 0%
where the time goes in v1:
time: 121 us
  Pallas kernels  99 us (82%)
  blocking collectives  16.2 us (13%)
  local copies, waits for them, and re-layouts  2.51 us (2%)
  other arithmetic  2.12 us (2%)
    pallas_call x1, Pallas kernels, pair_elements(): pl.pallas_call(functools.partial(spectrum_kernel, side, constant), out_sh...  99 us
    all_to_all x1, blocking collectives, local(): lax.all_to_all(message, ('val', 'col'), split_axis=0, concat_axis=0, tile...  16.2 us

profile of v1, /device:TPU:0, one launch (start us, length us, event | category | flops | bytes accessed | tf_op | source)
XLA Modules:
  0.0 120.9 jit_solution(10272745533988417041)
XLA Ops:
  0.0 1.4 %fusion.9 = (f32[4096]{0:T(1024)}, s32[4096]{0:T(1024)}) fusion(s32[4096]{0:T(1024)} %param.15), kind=kLoop, calls=%fused_computation.17 | loop fusion | flops 110592 | bytes 49152 | tf_op jit(solution)/shard_map/convert_element_type | solution.py:282
  2.0 99.0 %shard_map.100 = bf16[8,4096]{1,0:T(8,128)(2,1)} custom-call(s32[4096]{0:T(1024)} %get-tuple-element.8.rows_ref, s32[4]{0:T(128)} %owner_ref.1, f32[1]{0:T(128)S(6)} %copy.31.val_energy_ref, f32[4]{0:T(128)} %energy_ref.1, f32[2,48,2304]{2,1,0:T(8,128)} %bitcast.27, f32[4,2,48,2304]{3,2,1,0:T(8,128)} %cond_hbm.1, ...), custom_call_target="tpu_custom_call" | custom-call | tf_op jit(solution)/shard_map/pallas_call | solution.py:287
  101.0 0.7 slice.17
  101.7 0.1 reshape.21
  101.8 0.9 broadcast_in_dim.7
  102.7 16.2 %all_to_all.5 = bf16[32,8,576]{2,1,0:T(8,128)(2,1)S(1)} all-to-all(bf16[32,8,576]{2,1,0:T(8,128)(2,1)S(1)} %bitcast.25), channel_id=1, replica_groups=mesh['val'=4,'col'=8] {'val','col'}, dimensions={0} | all-to-all | bytes 589824 | tf_op jit(solution)/shard_map/all_to_all | solution.py:327
  118.9 0.3 copy.27
  119.3 0.1 fusion.13
  119.4 0.2 slice.23
  119.6 0.1 copy.29
  119.7 0.1 copy.28
  119.8 0.2 convolution_bitcast_fusion.1
  120.0 0.2 convolution_bitcast_fusion
  120.2 0.7 maximum_negate_fusion
  (6 shorter events, 0.1 us)

commit v2 on v1

--- a/solution.py
+++ b/solution.py
@@ -59,11 +59,18 @@
     return lax.dot_general(left, right, (dims, ((), ())), preferred_element_type=F32)
 
 
-def spectrum_kernel(
-    side, scale_constant, rows_ref, owner_ref, val_energy_ref, energy_ref, store_ref, cond_hbm,
-    first_high_ref, first_low_ref, left_ref, picker_ref, kx_ref, out_ref,
-    grid_a, grid_b, spots, chosen, cond_ref, streams, mine, valence_ref,
-    send_sems, recv_sems, cond_sem,
+def turn(side, left_ref, block):
+    half = block.shape[1] // 2
+    high, low = split(block)
+    both = dot(left_ref[...], jnp.concatenate([high, low, high], 0))
+    real = both[:side, :half] + both[side:, half:]
+    imag = both[:side, half:] - both[side:, :half]
+    return real, imag
+
+
+def spread_kernel(
+    side, owner_ref, store_ref, cond_hbm, first_high_ref, first_low_ref, left_ref, grid_b,
+    grid_a, cond_ref, streams, mine, valence_ref, send_sems, recv_sems, cond_sem,
 ):
     bands = cond_ref.shape[0]
     pairs = bands // 2
@@ -163,16 +170,9 @@
             grid_a[lanes, pair * LANES : (pair + 1) * LANES] = result[:, :LANES]
             grid_a[lanes, half + pair * LANES : half + (pair + 1) * LANES] = result[:, LANES:]
 
-    def turn(block):
-        high, low = split(block)
-        both = dot(left_ref[...], jnp.concatenate([high, low, high], 0))
-        real = both[:side, :half] + both[side:, half:]
-        imag = both[:side, half:] - both[side:, :half]
-        return real, imag
-
     def last_axis(y):
         rows = pl.ds(pl.multiple_of(y * side, 8), side)
-        real, imag = turn(grid_a[rows, :])
+        real, imag = turn(side, left_ref, grid_a[rows, :])
         for pair in range(pairs):
             span = slice(pair * LANES, (pair + 1) * LANES)
             grid_b[pair, rows, :] = real[:, span]
@@ -215,17 +215,37 @@
             def _(y):
                 last_axis(y)
 
+    @pl.loop(0, chunks)
+    def _(k):
+        copy(0, k).wait_send()
+        final_copy(core, k).wait_send()
+
+        @pl.when(has_right)
+        def _():
+            copy(1, k).wait_send()
+
+        @pl.when(has_left)
+        def _():
+            copy(2, k).wait_send()
+
+
+def pick_kernel(
+    side, bands, scale_constant, rows_ref, val_energy_ref, energy_ref, grid_b, left_ref,
+    picker_ref, kx_ref, out_ref, spots, chosen,
+):
+    pairs = bands // 2
+
     @pl.loop(0, side)
     def _(kz):
         block = jnp.concatenate(
             [grid_b[part, pl.ds(kz, side, stride=side), :] for part in range(2 * pairs)], 1
         )
-        real, imag = turn(block)
+        real, imag = turn(side, left_ref, block)
         for pair in range(pairs):
             span = slice(pair * LANES, (pair + 1) * LANES)
-            base = kz * side
-            spots[pl.ds(base, side), pair, :] = real[:, span]
-            spots[pl.ds(base, side), pairs + pair, :] = imag[:, span]
+            base = kz * side * 8
+            spots[pl.ds(base + pair, side, stride=8), :] = real[:, span]
+            spots[pl.ds(base + pairs + pair, side, stride=8), :] = imag[:, span]
 
     count = out_ref.shape[1]
     chunk = 512
@@ -244,32 +264,21 @@
         @pl.loop(0, chunk // 32)
         def _(inner):
             for item in range(32):
-                chosen[inner * 32 + item] = spots[rows_ref[base + inner * 32 + item]]
+                spot = pl.multiple_of(rows_ref[base + inner * 32 + item] * 8, 8)
+                to = pl.multiple_of((inner * 32 + item) * 8, 8)
+                chosen[pl.ds(to, 8), :] = spots[pl.ds(spot, 8), :]
 
         where = pl.ds(pl.multiple_of(base, chunk), chunk)
         wanted = jnp.broadcast_to(kx_ref[:, where], (LANES, chunk)).T
         mask = wanted == lane
         total = jnp.zeros((chunk, LANES), F32)
         for part in range(2 * pairs):
-            value = jnp.where(mask, chosen[:, part, :], 0.0)
+            value = jnp.where(mask, chosen[pl.ds(part, chunk, stride=8), :], 0.0)
             high, low = split(value)
             table = picker_ref[part * LANES : (part + 1) * LANES, :]
             total += dot(high, table) + dot(low, table)
         values = total.T[: out_ref.shape[0], :]
         out_ref[:, where] = (values * scale[:, :1]).astype(BF16)
-
-    @pl.loop(0, chunks)
-    def _(k):
-        copy(0, k).wait_send()
-        final_copy(core, k).wait_send()
-
-        @pl.when(has_right)
-        def _():
-            copy(1, k).wait_send()
-
-        @pl.when(has_left)
-        def _():
-            copy(2, k).wait_send()
 
 
 def pair_elements(store, owner, val_energy, cond_bands, cond_energy, gvec_index):
@@ -284,16 +293,13 @@
     constant = total_bands ** (-0.25) * side ** (-1.5)
     vmem = pl.BlockSpec(memory_space=pltpu.VMEM)
     smem = pl.BlockSpec(memory_space=pltpu.SMEM)
-    return pl.pallas_call(
-        functools.partial(spectrum_kernel, side, constant),
-        out_shape=jax.ShapeDtypeStruct((2 * bands, count), BF16),
-        in_specs=[smem] * 4 + [vmem, pl.BlockSpec(memory_space=pl.ANY)] + [vmem] * 5,
+    grid = pl.pallas_call(
+        functools.partial(spread_kernel, side),
+        out_shape=jax.ShapeDtypeStruct((2 * pairs, plane, LANES), F32),
+        in_specs=[smem, vmem, pl.BlockSpec(memory_space=pl.ANY)] + [vmem] * 3,
         out_specs=vmem,
         scratch_shapes=[
             pltpu.VMEM((plane, 2 * pairs * LANES), F32),
-            pltpu.VMEM((2 * pairs, plane, LANES), F32),
-            pltpu.VMEM((plane, 2 * pairs, LANES), F32),
-            pltpu.VMEM((512, 2 * pairs, LANES), F32),
             pltpu.VMEM(cond_bands.shape, F32),
             pltpu.VMEM((3, 2, chunks, side, WIDTH), F32),
             pltpu.VMEM((chunks, side, WIDTH), F32),
@@ -303,12 +309,20 @@
             pltpu.SemaphoreType.DMA,
         ],
         compiler_params=pltpu.CompilerParams(
-            vmem_limit_bytes=60 * 1024 * 1024, collective_id=0, has_side_effects=True
+            vmem_limit_bytes=32 * 1024 * 1024, collective_id=0, has_side_effects=True
         ),
-    )(
-        spot, owner, val_energy, cond_energy, store, cond_bands,
-        first_high, first_low, left, picker(side, pairs), kx,
-    )
+    )(owner, store, cond_bands, first_high, first_low, left)
+    return pl.pallas_call(
+        functools.partial(pick_kernel, side, bands, constant),
+        out_shape=jax.ShapeDtypeStruct((2 * bands, count), BF16),
+        in_specs=[smem] * 3 + [vmem] * 4,
+        out_specs=vmem,
+        scratch_shapes=[
+            pltpu.VMEM((plane * 8, LANES), F32),
+            pltpu.VMEM((512 * 8, LANES), F32),
+        ],
+        compiler_params=pltpu.CompilerParams(vmem_limit_bytes=32 * 1024 * 1024),
+    )(spot, val_energy, cond_energy, grid, left, picker(side, pairs), kx)
 
 
 def local(valence_store, band_owner, valence_energy, cond_bands, cond_energy, gvec_index):

time: 121 us -> 120 us (level)
  Pallas kernels: 99 us -> 93.2 us
  local copies, waits for them, and re-layouts: 2.51 us -> 7.41 us
    unnamed x0 -> x16, local copies, waits for them, and re-layouts: none -> 6.41 us
    pallas_call x1 -> x2, Pallas kernels: 99 us -> 93.2 us  [the longest x1 72.1 us: pair_elements(): pl.pallas_call(functools.partial(spread_kernel, side), out_shape=jax.Shap...]
where the time goes in v2:
time: 120 us; the launch traced here: 119 us
  Pallas kernels  93.2 us (78%)
  blocking collectives  16.2 us (14%)
  local copies, waits for them, and re-layouts  7.41 us (6%)
  other arithmetic  1.53 us (1%)
    pallas_call x1, Pallas kernels, pair_elements(): pl.pallas_call(functools.partial(spread_kernel, side), out_shape=jax.Shap...  72.1 us
    pallas_call x1, Pallas kernels, pair_elements(): pl.pallas_call(functools.partial(pick_kernel, side, bands, constant), out...  21.1 us
    all_to_all x1, blocking collectives, local(): lax.all_to_all(message, ('val', 'col'), split_axis=0, concat_axis=0, tile...  16.2 us
    unnamed x16, local copies, waits for them, and re-layouts  6.41 us

profile of v2, /device:TPU:0, one launch (start us, length us, event | category | flops | bytes accessed | tf_op | source)
XLA Modules:
  0.0 119.5 jit_solution(4586349234100431932)
XLA Ops:
  0.7 0.0 copy-start.7
  0.7 0.8 fusion.9
  1.4 0.0 copy-start
  1.4 2.0 %copy-done = f32[4,2,48,2304]{3,2,1,0:T(8,128)S(1)} copy-done((f32[4,2,48,2304]{3,2,1,0:T(8,128)S(1)}, f32[4,2,48,2304]{3,2,1,0:T(8,128)}, u32[]{:S(2)}) %copy-start) | copy-done | bytes 3538968
  3.4 0.0 copy-start.1
  3.4 1.2 copy-done.1
  4.6 0.0 copy-start.2
  4.6 0.8 copy-done.2
  5.4 0.0 copy-start.4
  5.4 0.9 copy-done.4
  6.3 0.0 copy-start.5
  6.3 0.9 copy-done.5
  7.2 0.0 copy-start.6
  7.2 0.7 copy-done.6
  7.8 0.0 copy-start.3
  7.8 72.1 %shard_map.100.grid_b = f32[4,2304,128]{2,1,0:T(8,128)S(1)} custom-call(s32[4]{0:T(128)S(1)} %copy-done.6, f32[2,48,2304]{2,1,0:T(8,128)S(1)} %bitcast.21, f32[4,2,48,2304]{3,2,1,0:T(8,128)S(1)} %copy-done, bf16[192,256]{1,0:T(8,128)(2,1)S(1)} %copy-done.5, bf16[192,256]{1,0:T(8,128)(2,1)S(1)} %copy-done.4, bf16[96,144]{1,0:T(8,128)(2,1)S(1)} %copy-done.2), custom_call_target="tpu_custom_call" | custom-call | tf_op jit(solution)/shard_map/pallas_call | solution.py:296
  80.0 0.0 copy-done.7
  80.0 0.0 copy-done.3
  80.0 21.1 %shard_map.101 = bf16[8,4096]{1,0:T(8,128)(2,1)S(1)} custom-call(s32[4096]{0:T(1024)S(1)} %get-tuple-element.8.rows_ref, f32[1]{0:T(128)S(6)} %copy.31.val_energy_ref, f32[4]{0:T(128)S(1)} %copy-done.7, f32[4,2304,128]{2,1,0:T(8,128)S(1)} %shard_map.100.grid_b, bf16[96,144]{1,0:T(8,128)(2,1)S(1)} %copy-done.2, bf16[512,128]{1,0:T(8,128)(2,1)S(1)} %copy-done.3, ...), custom_call_target="tpu_custom_call" | custom-call | tf_op jit(solution)/shard_map/pallas_call | solution.py:315
  101.1 0.1 reshape.21
  101.3 16.2 %all_to_all.5 = bf16[32,8,576]{2,1,0:T(8,128)(2,1)S(1)} all-to-all(bf16[32,8,576]{2,1,0:T(8,128)(2,1)S(1)} %bitcast.28), channel_id=1, replica_groups=mesh['val'=4,'col'=8] {'val','col'}, dimensions={0} | all-to-all | bytes 589824 | tf_op jit(solution)/shard_map/all_to_all | solution.py:341
  117.5 0.3 copy.27
  117.9 0.1 fusion.13
  118.0 0.2 slice.24
  118.2 0.1 copy.29
  118.3 0.1 copy.28
  118.4 0.2 convolution_bitcast_fusion
  118.6 0.2 convolution_bitcast_fusion.1
  118.8 0.7 maximum_negate_fusion
  (8 shorter events, 0.1 us)
Async XLA Ops:
  0.7 79.3 %copy-start.7 = (f32[4]{0:T(128)S(1)}, f32[4]{0:T(128)}, u32[]{:S(2)}) copy-start(f32[4]{0:T(128)} %energy_ref.1) | copy-start | bytes 52
  1.4 2.0 %copy-start = (f32[4,2,48,2304]{3,2,1,0:T(8,128)S(1)}, f32[4,2,48,2304]{3,2,1,0:T(8,128)}, u32[]{:S(2)}) copy-start(f32[4,2,48,2304]{3,2,1,0:T(8,128)} %cond_hbm.1) | copy-start | bytes 10616836
  3.4 1.2 copy-start.1
  4.6 0.8 copy-start.2
  5.4 0.9 copy-start.4
  6.3 0.9 copy-start.5
  7.2 0.7 copy-start.6
  7.8 72.1 %copy-start.3 = (bf16[512,128]{1,0:T(8,128)(2,1)S(1)}, bf16[512,128]{1,0:T(8,128)(2,1)}, u32[]{:S(2)}) copy-start(bf16[512,128]{1,0:T(8,128)(2,1)} %constant.41.clone.picker_ref) | copy-start | bytes 393220

commit v3 on v2

--- a/solution.py
+++ b/solution.py
@@ -178,10 +178,9 @@
             grid_b[pair, rows, :] = real[:, span]
             grid_b[pairs + pair, rows, :] = imag[:, span]
 
-    lag = max(1, chips // 2)
-    near_left = chip < chips // 2
-    right_lag = jnp.where(near_left, 0, lag)
-    left_lag = lag - right_lag
+    right_lag = 2 * chip
+    left_lag = 2 * (chips - 1 - chip)
+    lag = jnp.maximum(right_lag, left_lag)
     cond_copy.wait()
 
     @pl.loop(0, chunks + lag + 1)
@@ -309,7 +308,7 @@
             pltpu.SemaphoreType.DMA,
         ],
         compiler_params=pltpu.CompilerParams(
-            vmem_limit_bytes=32 * 1024 * 1024, collective_id=0, has_side_effects=True
+            vmem_limit_bytes=60 * 1024 * 1024, collective_id=0, has_side_effects=True
         ),
     )(owner, store, cond_bands, first_high, first_low, left)
     return pl.pallas_call(
@@ -321,7 +320,7 @@
             pltpu.VMEM((plane * 8, LANES), F32),
             pltpu.VMEM((512 * 8, LANES), F32),
         ],
-        compiler_params=pltpu.CompilerParams(vmem_limit_bytes=32 * 1024 * 1024),
+        compiler_params=pltpu.CompilerParams(vmem_limit_bytes=60 * 1024 * 1024),
     )(spot, val_energy, cond_energy, grid, left, picker(side, pairs), kx)
 
 

time: 120 us -> 79.3 us (0.66)
  Pallas kernels: 93.2 us -> 57.8 us
  local copies, waits for them, and re-layouts: 7.41 us -> 2.52 us
    pallas_call x1, Pallas kernels: 72.1 us -> 34.5 us  [pair_elements(): pl.pallas_call(functools.partial(spread_kernel, side), out_shape=jax.Shap...]
    unnamed x16 -> x0, local copies, waits for them, and re-layouts: 6.41 us -> none
    pallas_call x1, Pallas kernels: 21.1 us -> 23.3 us  [pair_elements(): pl.pallas_call(functools.partial(pick_kernel, side, bands, constant), out...]
where the time goes in v3:
time: 79.3 us; the launch traced here: 79 us
  Pallas kernels  57.8 us (73%)
  blocking collectives  15.4 us (19%)
  local copies, waits for them, and re-layouts  2.52 us (3%)
  other arithmetic  2.13 us (3%)
    pallas_call x1, Pallas kernels, pair_elements(): pl.pallas_call(functools.partial(spread_kernel, side), out_shape=jax.Shap...  34.5 us
    pallas_call x1, Pallas kernels, pair_elements(): pl.pallas_call(functools.partial(pick_kernel, side, bands, constant), out...  23.3 us
    all_to_all x1, blocking collectives, local(): lax.all_to_all(message, ('val', 'col'), split_axis=0, concat_axis=0, tile...  15.4 us

profile of v3, /device:TPU:0, one launch (start us, length us, event | category | flops | bytes accessed | tf_op | source)
XLA Modules:
  0.0 79.0 jit_solution(10697189034307356070)
XLA Ops:
  0.7 1.4 %fusion.9 = (f32[4096]{0:T(1024)}, s32[4096]{0:T(1024)}) fusion(s32[4096]{0:T(1024)} %param.15), kind=kLoop, calls=%fused_computation.17 | loop fusion | flops 110592 | bytes 49152 | tf_op jit(solution)/shard_map/convert_element_type | solution.py:290
  2.0 34.5 %shard_map.100.grid_b = f32[4,2304,128]{2,1,0:T(8,128)} custom-call(s32[4]{0:T(128)} %owner_ref.1, f32[2,48,2304]{2,1,0:T(8,128)} %bitcast.27, f32[4,2,48,2304]{3,2,1,0:T(8,128)} %cond_hbm.1, bf16[192,256]{1,0:T(8,128)(2,1)} %constant.38.clone.first_high_ref, bf16[192,256]{1,0:T(8,128)(2,1)} %constant.39.clone.first_low_ref, ...), custom_call_target="tpu_custom_call" | custom-call | tf_op jit(solution)/shard_map/pallas_call | solution.py:295
  36.5 23.3 %shard_map.101 = bf16[8,4096]{1,0:T(8,128)(2,1)} custom-call(s32[4096]{0:T(1024)} %get-tuple-element.8.rows_ref, f32[1]{0:T(128)S(6)} %copy.31.val_energy_ref, f32[4]{0:T(128)} %energy_ref.1, f32[4,2304,128]{2,1,0:T(8,128)} %shard_map.100.grid_b, bf16[96,144]{1,0:T(8,128)(2,1)} %constant.40.clone.left_ref, bf16[512,128]{1,0:T(8,128)(2,1)} %constant.41.clone.picker_ref, ...), custom_call_target="tpu_custom_call" | custom-call | tf_op jit(solution)/shard_map/pallas_call | solution.py:314
  59.8 0.7 slice.21
  60.5 0.1 reshape.21
  60.6 0.9 %broadcast_in_dim.7 = bf16[4,8,8,512]{3,2,1,0:T(8,128)(2,1)S(1)} broadcast(bf16[8,8,512]{2,1,0:T(8,128)(2,1)} %bitcast.28), dimensions={1,2,3} | broadcast | bytes 327680 | tf_op jit(solution)/shard_map/broadcast_in_dim | solution.py:336
  61.5 15.4 %all_to_all.5 = bf16[32,8,576]{2,1,0:T(8,128)(2,1)S(1)} all-to-all(bf16[32,8,576]{2,1,0:T(8,128)(2,1)S(1)} %bitcast.25), channel_id=1, replica_groups=mesh['val'=4,'col'=8] {'val','col'}, dimensions={0} | all-to-all | bytes 589824 | tf_op jit(solution)/shard_map/all_to_all | solution.py:340
  77.0 0.3 copy.27
  77.3 0.1 fusion.13
  77.4 0.2 slice.24
  77.7 0.1 copy.29
  77.8 0.1 copy.28
  77.9 0.2 convolution_bitcast_fusion
  78.1 0.2 convolution_bitcast_fusion.1
  78.2 0.7 maximum_negate_fusion
  (6 shorter events, 0.1 us)

commit v4 on v3

--- a/solution.py
+++ b/solution.py
@@ -246,8 +246,8 @@
             spots[pl.ds(base + pair, side, stride=8), :] = real[:, span]
             spots[pl.ds(base + pairs + pair, side, stride=8), :] = imag[:, span]
 
-    count = out_ref.shape[1]
-    chunk = 512
+    n_val, n_col = out_ref.shape[0], out_ref.shape[1]
+    chunk = out_ref.shape[3] - ROW_DEV
     row = lax.broadcasted_iota(jnp.int32, (2 * bands, LANES), 0) % bands
     energy = jnp.zeros((2 * bands, LANES), F32)
     for band in range(bands):
@@ -256,7 +256,7 @@
     lane = lax.broadcasted_iota(jnp.int32, (1, LANES), 1)
     lane = jnp.where(lane < side, lane, jnp.where(lane < 2 * side, lane - side, -1)).astype(F32)
 
-    @pl.loop(0, count // chunk)
+    @pl.loop(0, n_col)
     def _(step):
         base = step * chunk
 
@@ -276,8 +276,15 @@
             high, low = split(value)
             table = picker_ref[part * LANES : (part + 1) * LANES, :]
             total += dot(high, table) + dot(low, table)
-        values = total.T[: out_ref.shape[0], :]
-        out_ref[:, where] = (values * scale[:, :1]).astype(BF16)
+        values = (total.T[: 2 * bands, :] * scale[:, :1]).astype(BF16)
+        for index in range(n_val):
+            out_ref[index, step, :, :chunk] = values
+
+            @pl.when(step == index * ROW_DEV // chunk)
+            def _(index=index):
+                offset = index * ROW_DEV % chunk
+                for target in range(n_col):
+                    out_ref[index, target, :, chunk:] = values[:, offset : offset + ROW_DEV]
 
 
 def pair_elements(store, owner, val_energy, cond_bands, cond_energy, gvec_index):
@@ -288,7 +295,9 @@
     first_high, first_low, left = tables(side)
     spot = gvec_index % side * side + gvec_index // side % side
     kx = (gvec_index // plane).astype(F32)[None, :]
-    total_bands = bands * lax.axis_size("col") * lax.axis_size("val")
+    n_val, n_col = lax.axis_size("val"), lax.axis_size("col")
+    cols = count // n_col
+    total_bands = bands * n_col * n_val
     constant = total_bands ** (-0.25) * side ** (-1.5)
     vmem = pl.BlockSpec(memory_space=pltpu.VMEM)
     smem = pl.BlockSpec(memory_space=pltpu.SMEM)
@@ -313,12 +322,12 @@
     )(owner, store, cond_bands, first_high, first_low, left)
     return pl.pallas_call(
         functools.partial(pick_kernel, side, bands, constant),
-        out_shape=jax.ShapeDtypeStruct((2 * bands, count), BF16),
+        out_shape=jax.ShapeDtypeStruct((n_val, n_col, 2 * bands, cols + ROW_DEV), BF16),
         in_specs=[smem] * 3 + [vmem] * 4,
         out_specs=vmem,
         scratch_shapes=[
             pltpu.VMEM((plane * 8, LANES), F32),
-            pltpu.VMEM((512 * 8, LANES), F32),
+            pltpu.VMEM((cols * 8, LANES), F32),
         ],
         compiler_params=pltpu.CompilerParams(vmem_limit_bytes=60 * 1024 * 1024),
     )(spot, val_energy, cond_energy, grid, left, picker(side, pairs), kx)
@@ -327,16 +336,11 @@
 def local(valence_store, band_owner, valence_energy, cond_bands, cond_energy, gvec_index):
     bands, _, side, plane = cond_bands.shape
     n_val, n_col = lax.axis_size("val"), lax.axis_size("col")
-    picked = pair_elements(
+    message = pair_elements(
         valence_store[0, 0], band_owner, valence_energy, cond_bands, cond_energy, gvec_index
     )
-    count = picked.shape[1]
-    cols = count // n_col
-    columns = picked.reshape(2 * bands, n_col, cols).transpose(1, 0, 2)
-    columns = jnp.broadcast_to(columns[None], (n_val, n_col, 2 * bands, cols))
-    rows = picked[:, : ROW_DEV * n_val].reshape(2 * bands, n_val, ROW_DEV).transpose(1, 0, 2)
-    rows = jnp.broadcast_to(rows[:, None], (n_val, n_col, 2 * bands, ROW_DEV))
-    message = jnp.concatenate([columns, rows], 3).reshape(n_val * n_col, 2 * bands, cols + ROW_DEV)
+    cols = message.shape[3] - ROW_DEV
+    message = message.reshape(n_val * n_col, 2 * bands, cols + ROW_DEV)
     message = lax.all_to_all(message, ("val", "col"), split_axis=0, concat_axis=0, tiled=True)
     message = message.reshape(n_val * n_col, 2, bands, cols + ROW_DEV).transpose(1, 0, 2, 3)
     message = message.reshape(2, n_val * n_col * bands, cols + ROW_DEV)

time: 79.3 us -> 78.1 us (0.985)
  local copies, waits for them, and re-layouts: 2.52 us -> 0.87 us
    broadcast_in_dim x2 -> x0, local copies, waits for them, and re-layouts: 0.87 us -> none  [the longest x1 0.86 us: local(): columns = jnp.broadcast_to(columns[None], (n_val, n_col, 2 * bands, cols))]
where the time goes in v4:
time: 78.1 us; the launch traced here: 77.7 us
  Pallas kernels  58.1 us (74%)
  blocking collectives  15.6 us (20%)
  other arithmetic  2.1 us (3%)
  local copies, waits for them, and re-layouts  0.87 us (1%)
    pallas_call x1, Pallas kernels, pair_elements(): pl.pallas_call(functools.partial(spread_kernel, side), out_shape=jax.Shap...  34.5 us
    pallas_call x1, Pallas kernels, pair_elements(): pl.pallas_call(functools.partial(pick_kernel, side, bands, constant), out...  23.6 us
    all_to_all x1, blocking collectives, local(): lax.all_to_all(message, ('val', 'col'), split_axis=0, concat_axis=0, tile...  15.6 us

profile of v4, /device:TPU:0, one launch (start us, length us, event | category | flops | bytes accessed | tf_op | source)
XLA Modules:
  0.0 77.7 jit_solution(8487668762406276979)
XLA Ops:
  0.7 1.4 %fusion.9 = (f32[4096]{0:T(1024)}, s32[4096]{0:T(1024)}) fusion(s32[4096]{0:T(1024)} %param.15), kind=kLoop, calls=%fused_computation.16 | loop fusion | flops 110592 | bytes 49152 | tf_op jit(solution)/shard_map/convert_element_type | solution.py:297
  2.0 34.5 %shard_map.100.grid_b = f32[4,2304,128]{2,1,0:T(8,128)} custom-call(s32[4]{0:T(128)} %owner_ref.1, f32[2,48,2304]{2,1,0:T(8,128)} %bitcast.23, f32[4,2,48,2304]{3,2,1,0:T(8,128)} %cond_hbm.1, bf16[192,256]{1,0:T(8,128)(2,1)} %constant.38.clone.first_high_ref, bf16[192,256]{1,0:T(8,128)(2,1)} %constant.39.clone.first_low_ref, ...), custom_call_target="tpu_custom_call" | custom-call | tf_op jit(solution)/shard_map/pallas_call | solution.py:304
  36.5 23.6 %shard_map.101 = bf16[4,8,8,576]{3,2,1,0:T(8,128)(2,1)} custom-call(s32[4096]{0:T(1024)} %get-tuple-element.8.rows_ref, f32[1]{0:T(128)S(6)} %copy.28.val_energy_ref, f32[4]{0:T(128)} %energy_ref.1, f32[4,2304,128]{2,1,0:T(8,128)} %shard_map.100.grid_b, bf16[96,144]{1,0:T(8,128)(2,1)} %constant.40.clone.left_ref, ...), custom_call_target="tpu_custom_call" | custom-call | tf_op jit(solution)/shard_map/pallas_call | solution.py:323
  60.1 15.6 %all_to_all.5 = bf16[32,8,576]{2,1,0:T(8,128)(2,1)S(1)} all-to-all(bf16[32,8,576]{2,1,0:T(8,128)(2,1)} %bitcast.21), channel_id=1, replica_groups=mesh['val'=4,'col'=8] {'val','col'}, dimensions={0} | all-to-all | bytes 589824 | tf_op jit(solution)/shard_map/all_to_all | solution.py:344
  75.8 0.3 copy.24
  76.1 0.1 fusion.13
  76.2 0.2 slice.19
  76.4 0.1 copy.26
  76.5 0.1 copy.25
  76.6 0.2 convolution_bitcast_fusion
  76.8 0.2 convolution_bitcast_fusion.1
  77.0 0.7 maximum_negate_fusion
  (3 shorter events, 0.1 us)
